TPU v7x, 32 devices: a whole 2x2x4 slice. The times are simulated.
32 devices in a mesh: groups: 2 (over y), wide: 8 (over z, x), narrow: 2 (over core).
Axes of the slice: x: 2, y: 2, z: 4, core: 2. Of those that a mesh axis runs over, the one named last changes fastest.
Arguments:
- inputs: bfloat16 [8192, 1024], P(('groups', 'wide', 'narrow')), parts along dimension 0, may hold values from -6 to 6
- filter_taps: bfloat16 [4096, 1024], P(('wide', 'narrow')), may hold values from -6 to 6
- grad_out: bfloat16 [8192, 1024], P(('groups', 'wide', 'narrow')), parts along dimension 0, may hold values from -6 to 6
Outputs:
- outputs: bfloat16 [8192, 1024], P(('groups', 'wide', 'narrow')), parts along dimension 0
- grad_inputs: bfloat16 [8192, 1024], P(('groups', 'wide', 'narrow')), parts along dimension 0
- grad_taps: bfloat16 [8192, 1024], P(('groups', 'wide', 'narrow')), parts along dimension 0
There are 2 independent parts, one for each index of `groups`. A program takes and returns all parts, laid end to end along the dimension named above; an argument that names none is the same for every part. Nothing has to cross between parts.
All inputs are finite; a program needn't handle non-finite values.
Results may differ from a plain program's by a relative error of at most 0.008.
Values may be sent and summed in bfloat16 or wider, within the bound.
A program may use at most 64 MiB of HBM per device.

v0:
```python
import math
import jax
import jax.numpy as jnp
from jax import lax
from jax.sharding import PartitionSpec as P


def partner_2(value, axis, distance):
    mask = 2**distance
    pairs = [(source, source ^ mask) for source in range(lax.axis_size(axis))]
    return lax.ppermute(value, axis, pairs)


def on_device(inputs, filter_taps, grad_out):
    span_count = lax.axis_size("wide")
    blocksize = inputs.shape[0]
    channels = inputs.shape[1]
    shares = channels // span_count
    row_count = span_count * shares
    seq_len = span_count * 2 * blocksize
    parity = lax.axis_index("narrow")
    signed = (1 - 2 * parity).astype(jnp.float32)
    counter = jnp.arange(span_count, dtype=jnp.int32)
    long_angles = (counter[:, None] * counter[None, :] % span_count).astype(jnp.float32) * (
        2.0 * math.pi / span_count
    )
    long_cos = jnp.cos(long_angles)
    long_sin = jnp.sin(long_angles)
    long_forward = jnp.concatenate([long_cos, -long_sin], axis=0).astype(jnp.bfloat16)
    long_inverse = jnp.concatenate([long_cos, -long_sin], axis=1).astype(jnp.bfloat16)
    positions = jnp.arange(blocksize, dtype=jnp.int32)

    def first_section(pieces, twist_cos, twist_sin):
        share_count = pieces.shape[1]
        lane_count = pieces.shape[2]
        flatten = pieces.reshape(span_count, share_count * lane_count)
        mixture = jnp.dot(long_forward, flatten, preferred_element_type=jnp.float32)
        mixture = mixture.reshape(2, span_count, share_count, lane_count)
        real_part = mixture[0] * twist_cos + mixture[1] * twist_sin
        imag_part = mixture[1] * twist_cos - mixture[0] * twist_sin
        return jnp.stack([real_part, imag_part]).astype(jnp.bfloat16)

    def long_back(combined_re, combined_im, twist_cos, twist_sin):
        merged_re = combined_re * twist_cos - combined_im * twist_sin
        merged_im = combined_im * twist_cos + combined_re * twist_sin
        share_count = combined_re.shape[1]
        lane_count = combined_re.shape[2]
        stacked = (
            jnp.stack([merged_re, merged_im])
            .astype(jnp.bfloat16)
            .reshape(2 * span_count, share_count * lane_count)
        )
        summed = jnp.dot(long_inverse, stacked, preferred_element_type=jnp.float32) * (
            1.0 / seq_len
        )
        return summed.astype(jnp.bfloat16).reshape(span_count, share_count, lane_count)

    block_product = positions[:, None] * (2 * positions[None, :] + parity) % (2 * blocksize)
    block_angles = block_product.astype(jnp.float32) * (math.pi / blocksize)
    block_cos = jnp.cos(block_angles)
    block_sin = jnp.sin(block_angles)
    forward_mat = jnp.concatenate(
        [
            jnp.concatenate([block_cos, -block_sin], axis=1),
            jnp.concatenate([block_sin, block_cos], axis=1),
        ],
        axis=0,
    ).astype(jnp.bfloat16)
    cos_turned = jnp.transpose(block_cos)
    sin_turned = jnp.transpose(block_sin)
    inverse_mat = jnp.concatenate(
        [
            jnp.concatenate([cos_turned, sin_turned], axis=1),
            jnp.concatenate([-sin_turned, cos_turned], axis=1),
        ],
        axis=0,
    ).astype(jnp.bfloat16)
    twist_product = (parity * blocksize + positions)[None, None, :] * counter[:, None, None]
    twist_angles = twist_product.astype(jnp.float32) * (2.0 * math.pi / seq_len)
    twist_cos = jnp.cos(twist_angles)
    twist_sin = jnp.sin(twist_angles)

    def section_pairs(pieces):
        return first_section(pieces, twist_cos, twist_sin)

    def spectrum(signal):
        arranged = jnp.transpose(signal).reshape(span_count, shares, blocksize)
        twisted = section_pairs(
            lax.all_to_all(arranged, "wide", split_axis=0, concat_axis=0, tiled=True)
        )
        partner = partner_2(twisted, "narrow", 0)
        paired = (signed * twisted.astype(jnp.float32) + partner.astype(jnp.float32)).astype(
            jnp.bfloat16
        )
        joined = jnp.concatenate(
            [paired[0].reshape(row_count, blocksize), paired[1].reshape(row_count, blocksize)],
            axis=1,
        )
        return jnp.dot(joined, forward_mat, preferred_element_type=jnp.float32)

    def invert(spectrum_in):
        unfolded = jnp.dot(spectrum_in, inverse_mat, preferred_element_type=jnp.float32).astype(
            jnp.bfloat16
        )
        partner = partner_2(unfolded, "narrow", 0)
        combined = signed * unfolded.astype(jnp.float32) + partner.astype(jnp.float32)
        comb_re = combined[:, :blocksize].reshape(span_count, shares, blocksize)
        comb_im = combined[:, blocksize:].reshape(span_count, shares, blocksize)
        arranged = long_back(comb_re, comb_im, twist_cos, twist_sin)
        returned = lax.all_to_all(arranged, "wide", split_axis=0, concat_axis=1, tiled=True)
        return jnp.transpose(returned.reshape(channels, blocksize))

    def product(left_side, right_side, conjugate, factor):
        left_re = left_side[..., :blocksize]
        left_im = left_side[..., blocksize:]
        right_re = right_side[..., :blocksize]
        right_im = right_side[..., blocksize:]
        if conjugate:
            real_part = left_re * right_re + left_im * right_im
            imag_part = left_re * right_im - left_im * right_re
        else:
            real_part = left_re * right_re - left_im * right_im
            imag_part = left_re * right_im + left_im * right_re
        return (jnp.concatenate([real_part, imag_part], axis=-1) * factor).astype(jnp.bfloat16)

    kernel_scale = 1.0 / math.sqrt(seq_len)
    input_spectrum = spectrum(inputs)
    kernel_spectrum = spectrum(filter_taps) * kernel_scale
    outputs = invert(product(kernel_spectrum, input_spectrum, False, 1.0))
    grad_spectrum = spectrum(grad_out)
    grad_inputs = invert(product(kernel_spectrum, grad_spectrum, True, 1.0))
    grad_taps = invert(product(input_spectrum, grad_spectrum, True, kernel_scale))
    return (outputs, grad_inputs, grad_taps)


def solution(mesh):
    in_specs = (
        P(("groups", "wide", "narrow"), None),
        P(("wide", "narrow"), None),
        P(("groups", "wide", "narrow"), None),
    )
    out_specs = (
        P(("groups", "wide", "narrow"), None),
        P(("groups", "wide", "narrow"), None),
        P(("groups", "wide", "narrow"), None),
    )
    return jax.shard_map(
        on_device, mesh=mesh, in_specs=in_specs, out_specs=out_specs, check_vma=False
    )
```

profile of v0, /device:TPU:0, one launch (start us, length us, event | category | flops | bytes accessed | tf_op | source)
XLA Modules:
  0.0 144.9 jit_solution(16948435035127631216)
XLA Ops:
  0.7 2.1 %copy.61 = bf16[1024,256]{1,0:T(8,128)(2,1)} copy(bf16[1024,256]{0,1:T(8,128)(2,1)} %bitcast.84) | data formatting | bytes 1048576 | tf_op jit(solution)/shard_map/reshape | solution.py:87
  2.8 7.3 %all-to-all-start.1 = ((bf16[8,128,256]{2,1,0:T(8,128)(2,1)}), bf16[8,128,256]{2,1,0:T(8,128)(2,1)S(1)}, u32[]{:S(2)}, u32[]{:S(2)}) async-start(bf16[8,128,256]{2,1,0:T(8,128)(2,1)} %bitcast.7), calls=%async_computation.1 | async-start | bytes 1048576 | tf_op jit(solution)/shard_map/all_to_all | solution.py:89
  10.0 1.0 copy.60
  11.0 13.5 %all-to-all-done.1 = bf16[8,128,256]{2,1,0:T(8,128)(2,1)S(1)} async-done(((bf16[8,128,256]{2,1,0:T(8,128)(2,1)}), bf16[8,128,256]{2,1,0:T(8,128)(2,1)S(1)}, u32[]{:S(2)}, u32[]{:S(2)}) %all-to-all-start.1) | async-done | bytes 524320 | tf_op jit(solution)/shard_map/all_to_all | solution.py:89
  24.5 3.6 %all-to-all-start = ((bf16[8,128,256]{2,1,0:T(8,128)(2,1)}), bf16[8,128,256]{2,1,0:T(8,128)(2,1)S(1)}, u32[]{:S(2)}, u32[]{:S(2)}) async-start(bf16[8,128,256]{2,1,0:T(8,128)(2,1)} %bitcast.1), calls=%async_computation | async-start | bytes 1048576 | tf_op jit(solution)/shard_map/all_to_all | solution.py:89
  28.2 1.0 copy.62
  29.2 13.7 %all-to-all-done = bf16[8,128,256]{2,1,0:T(8,128)(2,1)S(1)} async-done(((bf16[8,128,256]{2,1,0:T(8,128)(2,1)}), bf16[8,128,256]{2,1,0:T(8,128)(2,1)S(1)}, u32[]{:S(2)}, u32[]{:S(2)}) %all-to-all-start) | async-done | bytes 524320 | tf_op jit(solution)/shard_map/all_to_all | solution.py:89
  42.8 3.6 %all-to-all-start.3 = ((bf16[8,128,256]{2,1,0:T(8,128)(2,1)}), bf16[8,128,256]{2,1,0:T(8,128)(2,1)S(1)}, u32[]{:S(2)}, u32[]{:S(2)}) async-start(bf16[8,128,256]{2,1,0:T(8,128)(2,1)} %bitcast.18), calls=%async_computation.3 | async-start | bytes 1048576 | tf_op jit(solution)/shard_map/all_to_all | solution.py:89
  47.2 13.9 %all-to-all-done.3 = bf16[8,128,256]{2,1,0:T(8,128)(2,1)S(1)} async-done(((bf16[8,128,256]{2,1,0:T(8,128)(2,1)}), bf16[8,128,256]{2,1,0:T(8,128)(2,1)S(1)}, u32[]{:S(2)}, u32[]{:S(2)}) %all-to-all-start.3) | async-done | bytes 524320 | tf_op jit(solution)/shard_map/all_to_all | solution.py:89
  61.4 0.4 fusion.47
  62.0 0.4 fusion.49
  62.5 0.4 fusion.48
  63.1 2.8 %add_convert_fusion.6 = (bf16[1,8,128,256]{3,2,1,0:T(8,128)(2,1)S(1)}, bf16[1,8,128,256]{3,2,1,0:T(8,128)(2,1)S(1)}, bf16[1,8,128,256]{3,2,1,0:T(8,128)(2,1)S(1)...) fusion(f32[1,8,128,256]{3,1,2,0:T(8,128)S(1)} %bitcast.62, ...), kind=kLoop, calls=%fused_computation.50 | loop fusion | flops 6291456 | bytes 9453568 | tf_op jit(solution)/shard_map/convert.6
  65.9 1.1 pad_maximum_fusion
  66.9 1.1 pad_maximum_fusion.1
  68.0 0.5 collective-permute-start.1
  68.5 2.5 %fusion.36 = (bf16[256,256]{1,0:T(8,128)(2,1)S(1)}, bf16[256,256]{1,0:T(8,128)(2,1)S(1)}, bf16[256,256]{1,0:T(8,128)(2,1)S(1)}, bf16[256,256]{1,0:T(8,128)(2,1)S...) fusion(s32[256]{0:T(256)S(1)} %multiply_add_fusion.1), kind=kLoop, calls=%fused_computation.85 | loop fusion | flops 2359296 | bytes 787456 | tf_op jit(solution)/shard_map/convert.15
  71.2 1.5 %add_convert_fusion.2 = bf16[2,8,128,256]{3,2,1,0:T(8,128)(2,1)S(1)} fusion(bf16[2,8,128,256]{3,2,1,0:T(8,128)(2,1)} %collective-permute-done, f32[]{:T(128)S(6)} %convert_element_type.121, bf16[1,8,128,256]{3,2,1,0:T(8,128)(2,1)S(1)} %get-tuple-element.47, bf16[1,8,128,256]{3,2,1,0:T(8,128)(2,1)S(1)} %get-tuple-element.48), kind=kLoop, calls=%fused_computation.13 | loop fusion | flops 3145728 | bytes 3145732 | tf_op jit(solution)/shard_map/convert_element_type | solution.py:92
  72.9 1.5 %add_convert_fusion.1 = bf16[2,8,128,256]{3,2,1,0:T(8,128)(2,1)S(1)} fusion(bf16[2,8,128,256]{3,2,1,0:T(8,128)(2,1)} %collective-permute-done.1, f32[]{:T(128)S(6)} %convert_element_type.121, bf16[1,8,128,256]{3,2,1,0:T(8,128)(2,1)S(1)} %get-tuple-element.45, bf16[1,8,128,256]{3,2,1,0:T(8,128)(2,1)S(1)} %get-tuple-element.46), kind=kLoop, calls=%fused_computation.12 | loop fusion | flops 3145728 | bytes 3145732 | tf_op jit(solution)/shard_map/convert_element_type | solution.py:92
  75.0 0.8 convolution_multiply_fusion.3
  75.8 0.8 fusion.8
  76.5 0.8 fusion.15
  77.3 1.0 multiply_add_fusion
  78.3 0.7 convolution_convert_fusion.2
  79.1 0.6 collective-permute-start.2
  79.6 0.7 convolution_convert_fusion
  80.5 0.5 add_convert_fusion.5
  81.0 0.8 convolution_convert_fusion.1
  81.8 0.5 collective-permute-start.4
  82.8 0.6 collective-permute-done.5
  83.9 1.0 collective-permute-done.4
  85.4 1.1 subtract_convert_fusion
  86.7 0.6 copy.68
  87.6 0.9 copy.58
  88.5 3.7 %all-to-all-start.5 = ((bf16[8,128,256]{2,1,0:T(8,128)(2,1)}), bf16[8,128,256]{2,1,0:T(8,128)(2,1)S(1)}, u32[]{:S(2)}, u32[]{:S(2)}) async-start(bf16[8,128,256]{2,1,0:T(8,128)(2,1)} %copy.58), calls=%async_computation.5 | async-start | bytes 1048576 | tf_op jit(solution)/shard_map/all_to_all | solution.py:110
  92.3 0.6 copy.65
  92.9 0.4 fusion
  93.2 0.9 copy.49
  94.1 13.1 %all-to-all-done.5 = bf16[8,128,256]{2,1,0:T(8,128)(2,1)S(1)} async-done(((bf16[8,128,256]{2,1,0:T(8,128)(2,1)}), bf16[8,128,256]{2,1,0:T(8,128)(2,1)S(1)}, u32[]{:S(2)}, u32[]{:S(2)}) %all-to-all-start.5) | async-done | bytes 524320 | tf_op jit(solution)/shard_map/all_to_all | solution.py:110
  107.2 3.6 %all-to-all-start.2 = ((bf16[8,128,256]{2,1,0:T(8,128)(2,1)}), bf16[8,128,256]{2,1,0:T(8,128)(2,1)S(1)}, u32[]{:S(2)}, u32[]{:S(2)}) async-start(bf16[8,128,256]{2,1,0:T(8,128)(2,1)} %copy.49), calls=%async_computation.2 | async-start | bytes 1048576 | tf_op jit(solution)/shard_map/all_to_all | solution.py:110
  111.0 0.6 copy.67
  111.9 0.9 copy.56
  112.8 12.7 %all-to-all-done.2 = bf16[8,128,256]{2,1,0:T(8,128)(2,1)S(1)} async-done(((bf16[8,128,256]{2,1,0:T(8,128)(2,1)}), bf16[8,128,256]{2,1,0:T(8,128)(2,1)S(1)}, u32[]{:S(2)}, u32[]{:S(2)}) %all-to-all-start.2) | async-done | bytes 524320 | tf_op jit(solution)/shard_map/all_to_all | solution.py:110
  125.5 3.6 %all-to-all-start.4 = ((bf16[8,128,256]{2,1,0:T(8,128)(2,1)}), bf16[8,128,256]{2,1,0:T(8,128)(2,1)S(1)}, u32[]{:S(2)}, u32[]{:S(2)}) async-start(bf16[8,128,256]{2,1,0:T(8,128)(2,1)} %copy.56), calls=%async_computation.4 | async-start | bytes 1048576 | tf_op jit(solution)/shard_map/all_to_all | solution.py:110
  129.2 1.0 copy.59
  130.2 1.0 copy.50
  131.2 12.7 %all-to-all-done.4 = bf16[8,128,256]{2,1,0:T(8,128)(2,1)S(1)} async-done(((bf16[8,128,256]{2,1,0:T(8,128)(2,1)}), bf16[8,128,256]{2,1,0:T(8,128)(2,1)S(1)}, u32[]{:S(2)}, u32[]{:S(2)}) %all-to-all-start.4) | async-done | bytes 524320 | tf_op jit(solution)/shard_map/all_to_all | solution.py:110
  143.9 1.0 copy.57
  (37 shorter events, 4.7 us)
Async XLA Ops:
  0.6 9.4 %copy-start = (bf16[256,1024]{1,0:T(8,128)(2,1)S(1)}, bf16[256,1024]{1,0:T(8,128)(2,1)}, u32[]{:S(2)}) copy-start(bf16[256,1024]{1,0:T(8,128)(2,1)} %param.4) | copy-start | bytes 1572868
  0.6 27.5 %copy-start.1 = (bf16[256,1024]{1,0:T(8,128)(2,1)S(1)}, bf16[256,1024]{1,0:T(8,128)(2,1)}, u32[]{:S(2)}) copy-start(bf16[256,1024]{1,0:T(8,128)(2,1)} %param.5) | copy-start | bytes 1572868
  2.8 21.7 %all-to-all-start.1 = ((bf16[8,128,256]{2,1,0:T(8,128)(2,1)}), bf16[8,128,256]{2,1,0:T(8,128)(2,1)S(1)}, u32[]{:S(2)}, u32[]{:S(2)}) async-start(bf16[8,128,256]{2,1,0:T(8,128)(2,1)} %bitcast.7), calls=%async_computation.1 | async-start | bytes 1048576 | tf_op jit(solution)/shard_map/all_to_all | solution.py:89
  24.5 18.3 %all-to-all-start = ((bf16[8,128,256]{2,1,0:T(8,128)(2,1)}), bf16[8,128,256]{2,1,0:T(8,128)(2,1)S(1)}, u32[]{:S(2)}, u32[]{:S(2)}) async-start(bf16[8,128,256]{2,1,0:T(8,128)(2,1)} %bitcast.1), calls=%async_computation | async-start | bytes 1048576 | tf_op jit(solution)/shard_map/all_to_all | solution.py:89
  42.8 18.3 %all-to-all-start.3 = ((bf16[8,128,256]{2,1,0:T(8,128)(2,1)}), bf16[8,128,256]{2,1,0:T(8,128)(2,1)S(1)}, u32[]{:S(2)}, u32[]{:S(2)}) async-start(bf16[8,128,256]{2,1,0:T(8,128)(2,1)} %bitcast.18), calls=%async_computation.3 | async-start | bytes 1048576 | tf_op jit(solution)/shard_map/all_to_all | solution.py:89
  66.9 4.3 %collective-permute-start = (bf16[2,8,128,256]{3,2,1,0:T(8,128)(2,1)}, bf16[2,8,128,256]{3,2,1,0:T(8,128)(2,1)}, u32[]{:S(2)}, u32[]{:S(2)}) collective-permute-start(bf16[2,8,128,256]{3,2,1,0:T(8,128)(2,1)} %pad_maximum_fusion), channel_id=1, source_target_pairs={{0,1},{1,0},{2,3},{3,2},{4,5},{5,4},{6,7},{7,6},{8,9},{9,8},{10,11... | collective-permute-start | bytes 3145736 | tf_op jit(solution)/shard_map/ppermute | solution.py:11
  68.0 4.9 %collective-permute-start.1 = (bf16[2,8,128,256]{3,2,1,0:T(8,128)(2,1)}, bf16[2,8,128,256]{3,2,1,0:T(8,128)(2,1)}, u32[]{:S(2)}, u32[]{:S(2)}) collective-permute-start(bf16[2,8,128,256]{3,2,1,0:T(8,128)(2,1)} %pad_maximum_fusion.1), channel_id=1, source_target_pairs={{0,1},{1,0},{2,3},{3,2},{4,5},{5,4},{6,7},{7,6},{8,9},{9,8},{10,11... | collective-permute-start | bytes 3145736 | tf_op jit(solution)/shard_map/ppermute | solution.py:11
  71.2 3.4 %collective-permute-start.3 = (bf16[2,8,128,256]{3,2,1,0:T(8,128)(2,1)S(1)}, bf16[2,8,128,256]{3,2,1,0:T(8,128)(2,1)S(1)}, u32[]{:S(2)}, u32[]{:S(2)}) collective-permute-start(bf16[2,8,128,256]{3,2,1,0:T(8,128)(2,1)S(1)} %pad_maximum_fusion.2), channel_id=1, source_target_pairs={{0,1},{1,0},{2,3},{3,2},{4,5},{5,4},{6,7},{7,6},{8,9},{9,8},{10,11... | collective-permute-start | bytes 3145736 | tf_op jit(solution)/shard_map/ppermute | solution.py:11
  79.1 3.2 %collective-permute-start.2 = (bf16[1024,512]{1,0:T(8,128)(2,1)S(1)}, bf16[1024,512]{1,0:T(8,128)(2,1)S(1)}, u32[]{:S(2)}, u32[]{:S(2)}) collective-permute-start(bf16[1024,512]{1,0:T(8,128)(2,1)S(1)} %convolution_convert_fusion.2), channel_id=1, source_target_pairs={{0,1},{1,0},{2,3},{3,2},{4,5},{5,4},{6,7},{7,6},{8,9},{9,8},{10,11... | collective-permute-start | bytes 3145736 | tf_op jit(solution)/shard_map/ppermute | solution.py:11
  80.4 3.0 %collective-permute-start.5 = (bf16[1024,512]{1,0:T(8,128)(2,1)S(1)}, bf16[1024,512]{1,0:T(8,128)(2,1)S(1)}, u32[]{:S(2)}, u32[]{:S(2)}) collective-permute-start(bf16[1024,512]{1,0:T(8,128)(2,1)S(1)} %convolution_convert_fusion), channel_id=1, source_target_pairs={{0,1},{1,0},{2,3},{3,2},{4,5},{5,4},{6,7},{7,6},{8,9},{9,8},{10,11... | collective-permute-start | bytes 3145736 | tf_op jit(solution)/shard_map/ppermute | solution.py:11
  81.8 3.1 %collective-permute-start.4 = (bf16[1024,512]{1,0:T(8,128)(2,1)S(1)}, bf16[1024,512]{1,0:T(8,128)(2,1)S(1)}, u32[]{:S(2)}, u32[]{:S(2)}) collective-permute-start(bf16[1024,512]{1,0:T(8,128)(2,1)S(1)} %convolution_convert_fusion.1), channel_id=1, source_target_pairs={{0,1},{1,0},{2,3},{3,2},{4,5},{5,4},{6,7},{7,6},{8,9},{9,8},{10,11... | collective-permute-start | bytes 3145736 | tf_op jit(solution)/shard_map/ppermute | solution.py:11
  88.5 18.7 %all-to-all-start.5 = ((bf16[8,128,256]{2,1,0:T(8,128)(2,1)}), bf16[8,128,256]{2,1,0:T(8,128)(2,1)S(1)}, u32[]{:S(2)}, u32[]{:S(2)}) async-start(bf16[8,128,256]{2,1,0:T(8,128)(2,1)} %copy.58), calls=%async_computation.5 | async-start | bytes 1048576 | tf_op jit(solution)/shard_map/all_to_all | solution.py:110
  107.2 18.3 %all-to-all-start.2 = ((bf16[8,128,256]{2,1,0:T(8,128)(2,1)}), bf16[8,128,256]{2,1,0:T(8,128)(2,1)S(1)}, u32[]{:S(2)}, u32[]{:S(2)}) async-start(bf16[8,128,256]{2,1,0:T(8,128)(2,1)} %copy.49), calls=%async_computation.2 | async-start | bytes 1048576 | tf_op jit(solution)/shard_map/all_to_all | solution.py:110
  125.5 18.3 %all-to-all-start.4 = ((bf16[8,128,256]{2,1,0:T(8,128)(2,1)}), bf16[8,128,256]{2,1,0:T(8,128)(2,1)S(1)}, u32[]{:S(2)}, u32[]{:S(2)}) async-start(bf16[8,128,256]{2,1,0:T(8,128)(2,1)} %copy.56), calls=%async_computation.4 | async-start | bytes 1048576 | tf_op jit(solution)/shard_map/all_to_all | solution.py:110
where the time goes:
time: 146 us; the launch traced here: 145 us
  waiting for transfers between devices  81.3 us (56%)
  starting transfers between devices  27.2 us (19%)
  other arithmetic  15 us (10%)
  local copies, waits for them, and re-layouts  13.6 us (9%)
  matrix products  6.81 us (5%)
    all_to_all x3, waiting for transfers between devices, spectrum(): lax.all_to_all(arranged, 'wide', split_axis=0, concat_axis=0, tiled=True)  41.1 us
    all_to_all x3, waiting for transfers between devices, invert(): lax.all_to_all(arranged, 'wide', split_axis=0, concat_axis=1, tiled=True)  38.5 us
    all_to_all x3, starting transfers between devices, spectrum(): lax.all_to_all(arranged, 'wide', split_axis=0, concat_axis=0, tiled=True)  14.5 us
    all_to_all x3, starting transfers between devices, invert(): lax.all_to_all(arranged, 'wide', split_axis=0, concat_axis=1, tiled=True)  10.9 us
    another operation x5, other arithmetic  6.97 us
    reshape x3, local copies, waits for them, and re-layouts, spectrum(): arranged = jnp.transpose(signal).reshape(span_count, shares, blocksize)  4.13 us
    convert_element_type x3, other arithmetic, spectrum(): (signed * twisted.astype(jnp.float32) + partner.astype(jnp.float32)).asty...  3.43 us
    reshape x3, local copies, waits for them, and re-layouts, invert(): return jnp.transpose(returned.reshape(channels, blocksize))  3 us
  transfers between devices with their start and end apart: 12, of which 8 were waited for; matrix products, arithmetic and copies ran while one was open for 13% of the time, Pallas kernels for 0%

commit v1 on v0

--- a/solution.py
+++ b/solution.py
@@ -3,6 +3,29 @@
 import jax.numpy as jnp
 from jax import lax
 from jax.sharding import PartitionSpec as P
+
+
+def in_blocks(array, dim, length):
+    lengths = array.shape
+    tiles = array.reshape(*lengths[:dim], length, lengths[dim] // length, *lengths[dim + 1 :])
+    return jnp.moveaxis(tiles, dim, 0)
+
+
+def in_order(tiles, dim):
+    tiles = jnp.moveaxis(tiles, 0, dim)
+    shape = tiles.shape
+    return tiles.reshape(*shape[:dim], shape[dim] * shape[dim + 1], *shape[dim + 2 :])
+
+
+def pairwise_exchange(shard, axis, split_dim, concat_dim):
+    length, here = (lax.axis_size(axis), lax.axis_index(axis))
+    parts = in_blocks(shard, split_dim, length)
+    done = [parts[here]]
+    for hop in range(1, length):
+        sent = parts[here ^ hop]
+        done.append(lax.ppermute(sent, axis, [(i, i ^ hop) for i in range(length)]))
+    parts = jnp.stack(done)[here ^ jnp.arange(length)]
+    return in_order(parts, concat_dim)
 
 
 def partner_2(value, axis, distance):
@@ -85,9 +108,7 @@
 
     def spectrum(signal):
         arranged = jnp.transpose(signal).reshape(span_count, shares, blocksize)
-        twisted = section_pairs(
-            lax.all_to_all(arranged, "wide", split_axis=0, concat_axis=0, tiled=True)
-        )
+        twisted = section_pairs(pairwise_exchange(arranged, "wide", 0, 0))
         partner = partner_2(twisted, "narrow", 0)
         paired = (signed * twisted.astype(jnp.float32) + partner.astype(jnp.float32)).astype(
             jnp.bfloat16

time: 146 us -> 161 us (1.10)
  starting transfers between devices: 27.2 us -> 52.6 us
  waiting for transfers between devices: 81.3 us -> 67 us
  local copies, waits for them, and re-layouts: 13.6 us -> 18.1 us
    all_to_all x3 -> x0, waiting for transfers between devices: 41.1 us -> none  [spectrum(): lax.all_to_all(arranged, 'wide', split_axis=0, concat_axis=0, tiled=True)]
    ppermute x0 -> x21, starting transfers between devices: none -> 38.4 us  [pairwise_exchange(): done.append(lax.ppermute(sent, axis, [(i, i ^ hop) for i in range(length)]))]
    ppermute x0 -> x21, waiting for transfers between devices: none -> 26.8 us  [pairwise_exchange(): done.append(lax.ppermute(sent, axis, [(i, i ^ hop) for i in range(length)]))]
    all_to_all x3 -> x0, starting transfers between devices: 14.5 us -> none  [spectrum(): lax.all_to_all(arranged, 'wide', split_axis=0, concat_axis=0, tiled=True)]
    reshape x3 -> x0, local copies, waits for them, and re-layouts: 4.13 us -> none  [spectrum(): arranged = jnp.transpose(signal).reshape(span_count, shares, blocksize)]
    unnamed x10 -> x30, local copies, waits for them, and re-layouts: 2.65 us -> 6.11 us
    gather x0 -> x3, local copies, waits for them, and re-layouts: none -> 1.74 us  [pairwise_exchange(): parts = jnp.stack(done)[here ^ jnp.arange(length)]]
    transpose x0 -> x3, local copies, waits for them, and re-layouts: none -> 1.73 us  [spectrum(): arranged = jnp.transpose(signal).reshape(span_count, shares, blocksize)]
  transfers between devices with their start and end apart: 12 -> 30, of which waited for: 8 -> 14; matrix products, arithmetic and copies ran while one was open for 13% -> 14% of each run, Pallas kernels for 0% -> 0%
where the time goes in v1:
time: 161 us
  waiting for transfers between devices  67 us (42%)
  starting transfers between devices  52.6 us (33%)
  local copies, waits for them, and re-layouts  18.1 us (11%)
  other arithmetic  14.8 us (9%)
  matrix products  6.81 us (4%)
    all_to_all x3, waiting for transfers between devices, invert(): lax.all_to_all(arranged, 'wide', split_axis=0, concat_axis=1, tiled=True)  38.5 us
    ppermute x21, starting transfers between devices, pairwise_exchange(): done.append(lax.ppermute(sent, axis, [(i, i ^ hop) for i in range(length)]))  38.4 us
    ppermute x21, waiting for transfers between devices, pairwise_exchange(): done.append(lax.ppermute(sent, axis, [(i, i ^ hop) for i in range(length)]))  26.8 us
    all_to_all x3, starting transfers between devices, invert(): lax.all_to_all(arranged, 'wide', split_axis=0, concat_axis=1, tiled=True)  12.4 us
    another operation x5, other arithmetic  6.79 us
    unnamed x30, local copies, waits for them, and re-layouts  6.11 us
    convert_element_type x3, other arithmetic, spectrum(): (signed * twisted.astype(jnp.float32) + partner.astype(jnp.float32)).asty...  3.43 us
  transfers between devices with their start and end apart: 30, of which 14 were waited for; matrix products, arithmetic and copies ran while one was open for 14% of the time, Pallas kernels for 0%

profile of v1, /device:TPU:0, one launch (start us, length us, event | category | flops | bytes accessed | tf_op | source)
XLA Modules:
  0.0 160.5 jit_solution(924927661435250348)
XLA Ops:
  0.7 1.3 copy.72
  2.8 6.0 %collective-permute-start.14 = (bf16[1,128,256]{2,1,0:T(8,128)(2,1)S(1)}, bf16[1,128,256]{2,1,0:T(8,128)(2,1)}, u32[]{:S(2)}, u32[]{:S(2)}) collective-permute-start(bf16[1,128,256]{2,1,0:T(8,128)(2,1)S(1)} %get-tuple-element.57), channel_id=1, source_target_pairs={{0,14},{2,12},{4,10},{6,8},{8,6},{10,4},{12,2},{14,0},{1,15},{3,13... | collective-permute-start | bytes 196616 | tf_op jit(solution)/shard_map/ppermute | solution.py:26
  9.7 1.9 %collective-permute-start.11 = (bf16[1,128,256]{2,1,0:T(8,128)(2,1)S(1)}, bf16[1,128,256]{2,1,0:T(8,128)(2,1)}, u32[]{:S(2)}, u32[]{:S(2)}) collective-permute-start(bf16[1,128,256]{2,1,0:T(8,128)(2,1)S(1)} %get-tuple-element.60), channel_id=1, source_target_pairs={{0,8},{2,10},{4,12},{6,14},{8,0},{10,2},{12,4},{14,6},{1,9},{3,11}... | collective-permute-start | bytes 196616 | tf_op jit(solution)/shard_map/ppermute | solution.py:26
  11.7 1.7 %collective-permute-start.8 = (bf16[1,128,256]{2,1,0:T(8,128)(2,1)}, bf16[1,128,256]{2,1,0:T(8,128)(2,1)}, u32[]{:S(2)}, u32[]{:S(2)}) collective-permute-start(bf16[1,128,256]{2,1,0:T(8,128)(2,1)} %get-tuple-element.63), channel_id=1, source_target_pairs={{0,2},{2,0},{4,6},{6,4},{8,10},{10,8},{12,14},{14,12},{1,3},{3,1},... | collective-permute-start | bytes 196616 | tf_op jit(solution)/shard_map/ppermute | solution.py:26
  14.1 2.4 %collective-permute-done.8 = bf16[1,128,256]{2,1,0:T(8,128)(2,1)} collective-permute-done((bf16[1,128,256]{2,1,0:T(8,128)(2,1)}, bf16[1,128,256]{2,1,0:T(8,128)(2,1)}, u32[]{:S(2)}, u32[]{:S(2)}) %collective-permute-start.8) | collective-permute-done | bytes 65568 | tf_op jit(solution)/shard_map/ppermute | solution.py:26
  16.4 1.3 collective-permute-start.9
  18.6 2.3 %collective-permute-done.9 = bf16[1,128,256]{2,1,0:T(8,128)(2,1)S(1)} collective-permute-done((bf16[1,128,256]{2,1,0:T(8,128)(2,1)S(1)}, bf16[1,128,256]{2,1,0:T(8,128)(2,1)S(1)}, u32[]{:S(2)}, u32[]{:S(2)}) %collective-permute-start.9) | collective-permute-done | bytes 65568 | tf_op jit(solution)/shard_map/ppermute | solution.py:26
  20.9 2.0 %collective-permute-start.10 = (bf16[1,128,256]{2,1,0:T(8,128)(2,1)S(1)}, bf16[1,128,256]{2,1,0:T(8,128)(2,1)S(1)}, u32[]{:S(2)}, u32[]{:S(2)}) collective-permute-start(bf16[1,128,256]{2,1,0:T(8,128)(2,1)S(1)} %get-tuple-element.61), channel_id=1, source_target_pairs={{0,6},{2,4},{4,2},{6,0},{8,14},{10,12},{12,10},{14,8},{1,7},{3,5},... | collective-permute-start | bytes 196616 | tf_op jit(solution)/shard_map/ppermute | solution.py:26
  22.9 3.2 %collective-permute-done.10 = bf16[1,128,256]{2,1,0:T(8,128)(2,1)S(1)} collective-permute-done((bf16[1,128,256]{2,1,0:T(8,128)(2,1)S(1)}, bf16[1,128,256]{2,1,0:T(8,128)(2,1)S(1)}, u32[]{:S(2)}, u32[]{:S(2)}) %collective-permute-start.10) | collective-permute-done | bytes 65568 | tf_op jit(solution)/shard_map/ppermute | solution.py:26
  26.1 4.9 %collective-permute-start.6 = (bf16[1,128,256]{2,1,0:T(8,128)(2,1)S(1)}, bf16[1,128,256]{2,1,0:T(8,128)(2,1)S(1)}, u32[]{:S(2)}, u32[]{:S(2)}) collective-permute-start(bf16[1,128,256]{2,1,0:T(8,128)(2,1)S(1)} %get-tuple-element.49), channel_id=1, source_target_pairs={{0,14},{2,12},{4,10},{6,8},{8,6},{10,4},{12,2},{14,0},{1,15},{3,13... | collective-permute-start | bytes 196616 | tf_op jit(solution)/shard_map/ppermute | solution.py:26
  31.0 0.8 bitcast_dynamic-update-slice_fusion.10
  32.5 0.8 bitcast_dynamic-update-slice_fusion.9
  33.3 2.4 %collective-permute-start.3 = (bf16[1,128,256]{2,1,0:T(8,128)(2,1)S(1)}, bf16[1,128,256]{2,1,0:T(8,128)(2,1)S(1)}, u32[]{:S(2)}, u32[]{:S(2)}) collective-permute-start(bf16[1,128,256]{2,1,0:T(8,128)(2,1)S(1)} %get-tuple-element.52), channel_id=1, source_target_pairs={{0,8},{2,10},{4,12},{6,14},{8,0},{10,2},{12,4},{14,6},{1,9},{3,11}... | collective-permute-start | bytes 196616 | tf_op jit(solution)/shard_map/ppermute | solution.py:26
  36.6 1.4 collective-permute-start
  38.8 2.0 %collective-permute-done = bf16[1,128,256]{2,1,0:T(8,128)(2,1)S(1)} collective-permute-done((bf16[1,128,256]{2,1,0:T(8,128)(2,1)S(1)}, bf16[1,128,256]{2,1,0:T(8,128)(2,1)S(1)}, u32[]{:S(2)}, u32[]{:S(2)}) %collective-permute-start) | collective-permute-done | bytes 65568 | tf_op jit(solution)/shard_map/ppermute | solution.py:26
  40.8 1.5 collective-permute-start.1
  42.3 2.8 %collective-permute-done.1 = bf16[1,128,256]{2,1,0:T(8,128)(2,1)S(1)} collective-permute-done((bf16[1,128,256]{2,1,0:T(8,128)(2,1)S(1)}, bf16[1,128,256]{2,1,0:T(8,128)(2,1)S(1)}, u32[]{:S(2)}, u32[]{:S(2)}) %collective-permute-start.1) | collective-permute-done | bytes 65568 | tf_op jit(solution)/shard_map/ppermute | solution.py:26
  45.1 2.3 %collective-permute-start.2 = (bf16[1,128,256]{2,1,0:T(8,128)(2,1)S(1)}, bf16[1,128,256]{2,1,0:T(8,128)(2,1)S(1)}, u32[]{:S(2)}, u32[]{:S(2)}) collective-permute-start(bf16[1,128,256]{2,1,0:T(8,128)(2,1)S(1)} %get-tuple-element.53), channel_id=1, source_target_pairs={{0,6},{2,4},{4,2},{6,0},{8,14},{10,12},{12,10},{14,8},{1,7},{3,5},... | collective-permute-start | bytes 196616 | tf_op jit(solution)/shard_map/ppermute | solution.py:26
  47.4 3.6 %collective-permute-done.2 = bf16[1,128,256]{2,1,0:T(8,128)(2,1)S(1)} collective-permute-done((bf16[1,128,256]{2,1,0:T(8,128)(2,1)S(1)}, bf16[1,128,256]{2,1,0:T(8,128)(2,1)S(1)}, u32[]{:S(2)}, u32[]{:S(2)}) %collective-permute-start.2) | collective-permute-done | bytes 65568 | tf_op jit(solution)/shard_map/ppermute | solution.py:26
  51.0 4.3 %collective-permute-start.23 = (bf16[1,128,256]{2,1,0:T(8,128)(2,1)S(1)}, bf16[1,128,256]{2,1,0:T(8,128)(2,1)S(1)}, u32[]{:S(2)}, u32[]{:S(2)}) collective-permute-start(bf16[1,128,256]{2,1,0:T(8,128)(2,1)S(1)} %get-tuple-element.41), channel_id=1, source_target_pairs={{0,14},{2,12},{4,10},{6,8},{8,6},{10,4},{12,2},{14,0},{1,15},{3,13... | collective-permute-start | bytes 196616 | tf_op jit(solution)/shard_map/ppermute | solution.py:26
  55.7 3.1 %collective-permute-start.20 = (bf16[1,128,256]{2,1,0:T(8,128)(2,1)S(1)}, bf16[1,128,256]{2,1,0:T(8,128)(2,1)S(1)}, u32[]{:S(2)}, u32[]{:S(2)}) collective-permute-start(bf16[1,128,256]{2,1,0:T(8,128)(2,1)S(1)} %get-tuple-element.44), channel_id=1, source_target_pairs={{0,8},{2,10},{4,12},{6,14},{8,0},{10,2},{12,4},{14,6},{1,9},{3,11}... | collective-permute-start | bytes 196616 | tf_op jit(solution)/shard_map/ppermute | solution.py:26
  58.9 1.1 collective-permute-start.17
  60.0 3.6 %collective-permute-done.17 = bf16[1,128,256]{2,1,0:T(8,128)(2,1)S(1)} collective-permute-done((bf16[1,128,256]{2,1,0:T(8,128)(2,1)S(1)}, bf16[1,128,256]{2,1,0:T(8,128)(2,1)S(1)}, u32[]{:S(2)}, u32[]{:S(2)}) %collective-permute-start.17) | collective-permute-done | bytes 65568 | tf_op jit(solution)/shard_map/ppermute | solution.py:26
  63.6 1.0 collective-permute-start.18
  64.7 3.2 %collective-permute-done.18 = bf16[1,128,256]{2,1,0:T(8,128)(2,1)S(1)} collective-permute-done((bf16[1,128,256]{2,1,0:T(8,128)(2,1)S(1)}, bf16[1,128,256]{2,1,0:T(8,128)(2,1)S(1)}, u32[]{:S(2)}, u32[]{:S(2)}) %collective-permute-start.18) | collective-permute-done | bytes 65568 | tf_op jit(solution)/shard_map/ppermute | solution.py:26
  67.9 1.5 collective-permute-start.19
  69.4 3.6 %collective-permute-done.19 = bf16[1,128,256]{2,1,0:T(8,128)(2,1)S(1)} collective-permute-done((bf16[1,128,256]{2,1,0:T(8,128)(2,1)S(1)}, bf16[1,128,256]{2,1,0:T(8,128)(2,1)S(1)}, u32[]{:S(2)}, u32[]{:S(2)}) %collective-permute-start.19) | collective-permute-done | bytes 65568 | tf_op jit(solution)/shard_map/ppermute | solution.py:26
  77.5 2.8 %add_convert_fusion.6 = (bf16[1,8,128,256]{3,2,1,0:T(8,128)(2,1)S(1)}, bf16[1,8,128,256]{3,2,1,0:T(8,128)(2,1)S(1)}, bf16[1,8,128,256]{3,2,1,0:T(8,128)(2,1)S(1)...) fusion(f32[1,8,128,256]{3,1,2,0:T(8,128)S(1)} %bitcast.193, ...), kind=kLoop, calls=%fused_computation.53 | loop fusion | flops 6291456 | bytes 9453568 | tf_op jit(solution)/shard_map/convert.6
  80.3 1.1 pad_maximum_fusion
  81.3 1.1 pad_maximum_fusion.1
  82.9 2.3 %fusion.36 = (bf16[256,256]{1,0:T(8,128)(2,1)S(1)}, bf16[256,256]{1,0:T(8,128)(2,1)S(1)}, bf16[256,256]{1,0:T(8,128)(2,1)S(1)}, bf16[256,256]{1,0:T(8,128)(2,1)S...) fusion(s32[256]{0:T(256)S(1)} %multiply_add_fusion.1), kind=kLoop, calls=%fused_computation.88 | loop fusion | flops 2359296 | bytes 787456 | tf_op jit(solution)/shard_map/convert.15
  85.4 1.5 add_convert_fusion.2
  87.1 1.5 add_convert_fusion.1
  91.5 1.0 multiply_add_fusion
  98.1 1.0 collective-permute-done.25
  99.6 1.1 subtract_convert_fusion
  101.8 0.9 copy.100
  102.7 5.2 %all-to-all-start.2 = ((bf16[8,128,256]{2,1,0:T(8,128)(2,1)}), bf16[8,128,256]{2,1,0:T(8,128)(2,1)S(1)}, u32[]{:S(2)}, u32[]{:S(2)}) async-start(bf16[8,128,256]{2,1,0:T(8,128)(2,1)} %copy.100), calls=%async_computation.2 | async-start | bytes 1048576 | tf_op jit(solution)/shard_map/all_to_all | solution.py:131
  108.9 0.9 copy.84
  109.8 13.1 %all-to-all-done.2 = bf16[8,128,256]{2,1,0:T(8,128)(2,1)S(1)} async-done(((bf16[8,128,256]{2,1,0:T(8,128)(2,1)}), bf16[8,128,256]{2,1,0:T(8,128)(2,1)S(1)}, u32[]{:S(2)}, u32[]{:S(2)}) %all-to-all-start.2) | async-done | bytes 524320 | tf_op jit(solution)/shard_map/all_to_all | solution.py:131
  122.9 3.6 %all-to-all-start = ((bf16[8,128,256]{2,1,0:T(8,128)(2,1)}), bf16[8,128,256]{2,1,0:T(8,128)(2,1)S(1)}, u32[]{:S(2)}, u32[]{:S(2)}) async-start(bf16[8,128,256]{2,1,0:T(8,128)(2,1)} %copy.84), calls=%async_computation | async-start | bytes 1048576 | tf_op jit(solution)/shard_map/all_to_all | solution.py:131
  127.6 0.9 copy.98
  128.5 12.7 %all-to-all-done = bf16[8,128,256]{2,1,0:T(8,128)(2,1)S(1)} async-done(((bf16[8,128,256]{2,1,0:T(8,128)(2,1)}), bf16[8,128,256]{2,1,0:T(8,128)(2,1)S(1)}, u32[]{:S(2)}, u32[]{:S(2)}) %all-to-all-start) | async-done | bytes 524320 | tf_op jit(solution)/shard_map/all_to_all | solution.py:131
  141.2 3.6 %all-to-all-start.1 = ((bf16[8,128,256]{2,1,0:T(8,128)(2,1)}), bf16[8,128,256]{2,1,0:T(8,128)(2,1)S(1)}, u32[]{:S(2)}, u32[]{:S(2)}) async-start(bf16[8,128,256]{2,1,0:T(8,128)(2,1)} %copy.98), calls=%async_computation.1 | async-start | bytes 1048576 | tf_op jit(solution)/shard_map/all_to_all | solution.py:131
  144.9 1.0 copy.101
  145.9 1.0 copy.85
  146.9 12.7 %all-to-all-done.1 = bf16[8,128,256]{2,1,0:T(8,128)(2,1)S(1)} async-done(((bf16[8,128,256]{2,1,0:T(8,128)(2,1)}), bf16[8,128,256]{2,1,0:T(8,128)(2,1)S(1)}, u32[]{:S(2)}, u32[]{:S(2)}) %all-to-all-start.1) | async-done | bytes 524320 | tf_op jit(solution)/shard_map/all_to_all | solution.py:131
  159.5 1.0 copy.99
  (104 shorter events, 23.0 us)
Async XLA Ops:
  0.6 12.8 %copy-start = (bf16[256,1024]{1,0:T(8,128)(2,1)S(1)}, bf16[256,1024]{1,0:T(8,128)(2,1)}, u32[]{:S(2)}) copy-start(bf16[256,1024]{1,0:T(8,128)(2,1)} %param.4) | copy-start | bytes 1572868
  0.7 13.1 %copy-start.1 = (bf16[256,1024]{1,0:T(8,128)(2,1)S(1)}, bf16[256,1024]{1,0:T(8,128)(2,1)}, u32[]{:S(2)}) copy-start(bf16[256,1024]{1,0:T(8,128)(2,1)} %param.5) | copy-start | bytes 1572868
  2.8 33.8 %collective-permute-start.14 = (bf16[1,128,256]{2,1,0:T(8,128)(2,1)S(1)}, bf16[1,128,256]{2,1,0:T(8,128)(2,1)}, u32[]{:S(2)}, u32[]{:S(2)}) collective-permute-start(bf16[1,128,256]{2,1,0:T(8,128)(2,1)S(1)} %get-tuple-element.57), channel_id=1, source_target_pairs={{0,14},{2,12},{4,10},{6,8},{8,6},{10,4},{12,2},{14,0},{1,15},{3,13... | collective-permute-start | bytes 196616 | tf_op jit(solution)/shard_map/ppermute | solution.py:26
  8.7 24.6 %collective-permute-start.13 = (bf16[1,128,256]{2,1,0:T(8,128)(2,1)S(1)}, bf16[1,128,256]{2,1,0:T(8,128)(2,1)}, u32[]{:S(2)}, u32[]{:S(2)}) collective-permute-start(bf16[1,128,256]{2,1,0:T(8,128)(2,1)S(1)} %get-tuple-element.58), channel_id=1, source_target_pairs={{0,12},{2,14},{4,8},{6,10},{8,4},{10,6},{12,0},{14,2},{1,13},{3,15... | collective-permute-start | bytes 196616 | tf_op jit(solution)/shard_map/ppermute | solution.py:26
  9.0 22.9 %collective-permute-start.12 = (bf16[1,128,256]{2,1,0:T(8,128)(2,1)S(1)}, bf16[1,128,256]{2,1,0:T(8,128)(2,1)}, u32[]{:S(2)}, u32[]{:S(2)}) collective-permute-start(bf16[1,128,256]{2,1,0:T(8,128)(2,1)S(1)} %get-tuple-element.59), channel_id=1, source_target_pairs={{0,10},{2,8},{4,14},{6,12},{8,2},{10,0},{12,6},{14,4},{1,11},{3,9}... | collective-permute-start | bytes 196616 | tf_op jit(solution)/shard_map/ppermute | solution.py:26
  9.7 21.2 %collective-permute-start.11 = (bf16[1,128,256]{2,1,0:T(8,128)(2,1)S(1)}, bf16[1,128,256]{2,1,0:T(8,128)(2,1)}, u32[]{:S(2)}, u32[]{:S(2)}) collective-permute-start(bf16[1,128,256]{2,1,0:T(8,128)(2,1)S(1)} %get-tuple-element.60), channel_id=1, source_target_pairs={{0,8},{2,10},{4,12},{6,14},{8,0},{10,2},{12,4},{14,6},{1,9},{3,11}... | collective-permute-start | bytes 196616 | tf_op jit(solution)/shard_map/ppermute | solution.py:26
  11.7 4.8 %collective-permute-start.8 = (bf16[1,128,256]{2,1,0:T(8,128)(2,1)}, bf16[1,128,256]{2,1,0:T(8,128)(2,1)}, u32[]{:S(2)}, u32[]{:S(2)}) collective-permute-start(bf16[1,128,256]{2,1,0:T(8,128)(2,1)} %get-tuple-element.63), channel_id=1, source_target_pairs={{0,2},{2,0},{4,6},{6,4},{8,10},{10,8},{12,14},{14,12},{1,3},{3,1},... | collective-permute-start | bytes 196616 | tf_op jit(solution)/shard_map/ppermute | solution.py:26
  13.7 2.8 %copy-start.2 = (bf16[1,128,256]{2,1,0:T(8,128)(2,1)S(1)}, bf16[1,128,256]{2,1,0:T(8,128)(2,1)}, u32[]{:S(2)}) copy-start(bf16[1,128,256]{2,1,0:T(8,128)(2,1)} %get-tuple-element.62) | copy-start | bytes 196612
  16.4 4.5 %collective-permute-start.9 = (bf16[1,128,256]{2,1,0:T(8,128)(2,1)S(1)}, bf16[1,128,256]{2,1,0:T(8,128)(2,1)S(1)}, u32[]{:S(2)}, u32[]{:S(2)}) collective-permute-start(bf16[1,128,256]{2,1,0:T(8,128)(2,1)S(1)} %copy-done.2), channel_id=1, source_target_pairs={{0,4},{2,6},{4,0},{6,2},{8,12},{10,14},{12,8},{14,10},{1,5},{3,7},... | collective-permute-start | bytes 196616 | tf_op jit(solution)/shard_map/ppermute | solution.py:26
  20.9 5.2 %collective-permute-start.10 = (bf16[1,128,256]{2,1,0:T(8,128)(2,1)S(1)}, bf16[1,128,256]{2,1,0:T(8,128)(2,1)S(1)}, u32[]{:S(2)}, u32[]{:S(2)}) collective-permute-start(bf16[1,128,256]{2,1,0:T(8,128)(2,1)S(1)} %get-tuple-element.61), channel_id=1, source_target_pairs={{0,6},{2,4},{4,2},{6,0},{8,14},{10,12},{12,10},{14,8},{1,7},{3,5},... | collective-permute-start | bytes 196616 | tf_op jit(solution)/shard_map/ppermute | solution.py:26
  26.1 32.8 %collective-permute-start.6 = (bf16[1,128,256]{2,1,0:T(8,128)(2,1)S(1)}, bf16[1,128,256]{2,1,0:T(8,128)(2,1)S(1)}, u32[]{:S(2)}, u32[]{:S(2)}) collective-permute-start(bf16[1,128,256]{2,1,0:T(8,128)(2,1)S(1)} %get-tuple-element.49), channel_id=1, source_target_pairs={{0,14},{2,12},{4,10},{6,8},{8,6},{10,4},{12,2},{14,0},{1,15},{3,13... | collective-permute-start | bytes 196616 | tf_op jit(solution)/shard_map/ppermute | solution.py:26
  30.9 24.8 %collective-permute-start.5 = (bf16[1,128,256]{2,1,0:T(8,128)(2,1)S(1)}, bf16[1,128,256]{2,1,0:T(8,128)(2,1)S(1)}, u32[]{:S(2)}, u32[]{:S(2)}) collective-permute-start(bf16[1,128,256]{2,1,0:T(8,128)(2,1)S(1)} %get-tuple-element.50), channel_id=1, source_target_pairs={{0,12},{2,14},{4,8},{6,10},{8,4},{10,6},{12,0},{14,2},{1,13},{3,15... | collective-permute-start | bytes 196616 | tf_op jit(solution)/shard_map/ppermute | solution.py:26
  31.9 23.5 %collective-permute-start.4 = (bf16[1,128,256]{2,1,0:T(8,128)(2,1)S(1)}, bf16[1,128,256]{2,1,0:T(8,128)(2,1)S(1)}, u32[]{:S(2)}, u32[]{:S(2)}) collective-permute-start(bf16[1,128,256]{2,1,0:T(8,128)(2,1)S(1)} %get-tuple-element.51), channel_id=1, source_target_pairs={{0,10},{2,8},{4,14},{6,12},{8,2},{10,0},{12,6},{14,4},{1,11},{3,9}... | collective-permute-start | bytes 196616 | tf_op jit(solution)/shard_map/ppermute | solution.py:26
  33.3 21.9 %collective-permute-start.3 = (bf16[1,128,256]{2,1,0:T(8,128)(2,1)S(1)}, bf16[1,128,256]{2,1,0:T(8,128)(2,1)S(1)}, u32[]{:S(2)}, u32[]{:S(2)}) collective-permute-start(bf16[1,128,256]{2,1,0:T(8,128)(2,1)S(1)} %get-tuple-element.52), channel_id=1, source_target_pairs={{0,8},{2,10},{4,12},{6,14},{8,0},{10,2},{12,4},{14,6},{1,9},{3,11}... | collective-permute-start | bytes 196616 | tf_op jit(solution)/shard_map/ppermute | solution.py:26
  36.6 4.3 %collective-permute-start = (bf16[1,128,256]{2,1,0:T(8,128)(2,1)S(1)}, bf16[1,128,256]{2,1,0:T(8,128)(2,1)S(1)}, u32[]{:S(2)}, u32[]{:S(2)}) collective-permute-start(bf16[1,128,256]{2,1,0:T(8,128)(2,1)S(1)} %get-tuple-element.55), channel_id=1, source_target_pairs={{0,2},{2,0},{4,6},{6,4},{8,10},{10,8},{12,14},{14,12},{1,3},{3,1},... | collective-permute-start | bytes 196616 | tf_op jit(solution)/shard_map/ppermute | solution.py:26
  40.8 4.3 %collective-permute-start.1 = (bf16[1,128,256]{2,1,0:T(8,128)(2,1)S(1)}, bf16[1,128,256]{2,1,0:T(8,128)(2,1)S(1)}, u32[]{:S(2)}, u32[]{:S(2)}) collective-permute-start(bf16[1,128,256]{2,1,0:T(8,128)(2,1)S(1)} %get-tuple-element.54), channel_id=1, source_target_pairs={{0,4},{2,6},{4,0},{6,2},{8,12},{10,14},{12,8},{14,10},{1,5},{3,7},... | collective-permute-start | bytes 196616 | tf_op jit(solution)/shard_map/ppermute | solution.py:26
  45.1 5.9 %collective-permute-start.2 = (bf16[1,128,256]{2,1,0:T(8,128)(2,1)S(1)}, bf16[1,128,256]{2,1,0:T(8,128)(2,1)S(1)}, u32[]{:S(2)}, u32[]{:S(2)}) collective-permute-start(bf16[1,128,256]{2,1,0:T(8,128)(2,1)S(1)} %get-tuple-element.53), channel_id=1, source_target_pairs={{0,6},{2,4},{4,2},{6,0},{8,14},{10,12},{12,10},{14,8},{1,7},{3,5},... | collective-permute-start | bytes 196616 | tf_op jit(solution)/shard_map/ppermute | solution.py:26
  51.0 23.9 %collective-permute-start.23 = (bf16[1,128,256]{2,1,0:T(8,128)(2,1)S(1)}, bf16[1,128,256]{2,1,0:T(8,128)(2,1)S(1)}, u32[]{:S(2)}, u32[]{:S(2)}) collective-permute-start(bf16[1,128,256]{2,1,0:T(8,128)(2,1)S(1)} %get-tuple-element.41), channel_id=1, source_target_pairs={{0,14},{2,12},{4,10},{6,8},{8,6},{10,4},{12,2},{14,0},{1,15},{3,13... | collective-permute-start | bytes 196616 | tf_op jit(solution)/shard_map/ppermute | solution.py:26
  55.3 17.8 %collective-permute-start.22 = (bf16[1,128,256]{2,1,0:T(8,128)(2,1)S(1)}, bf16[1,128,256]{2,1,0:T(8,128)(2,1)S(1)}, u32[]{:S(2)}, u32[]{:S(2)}) collective-permute-start(bf16[1,128,256]{2,1,0:T(8,128)(2,1)S(1)} %get-tuple-element.42), channel_id=1, source_target_pairs={{0,12},{2,14},{4,8},{6,10},{8,4},{10,6},{12,0},{14,2},{1,13},{3,15... | collective-permute-start | bytes 196616 | tf_op jit(solution)/shard_map/ppermute | solution.py:26
  55.4 17.7 %collective-permute-start.21 = (bf16[1,128,256]{2,1,0:T(8,128)(2,1)S(1)}, bf16[1,128,256]{2,1,0:T(8,128)(2,1)S(1)}, u32[]{:S(2)}, u32[]{:S(2)}) collective-permute-start(bf16[1,128,256]{2,1,0:T(8,128)(2,1)S(1)} %get-tuple-element.43), channel_id=1, source_target_pairs={{0,10},{2,8},{4,14},{6,12},{8,2},{10,0},{12,6},{14,4},{1,11},{3,9}... | collective-permute-start | bytes 196616 | tf_op jit(solution)/shard_map/ppermute | solution.py:26
  55.7 17.4 %collective-permute-start.20 = (bf16[1,128,256]{2,1,0:T(8,128)(2,1)S(1)}, bf16[1,128,256]{2,1,0:T(8,128)(2,1)S(1)}, u32[]{:S(2)}, u32[]{:S(2)}) collective-permute-start(bf16[1,128,256]{2,1,0:T(8,128)(2,1)S(1)} %get-tuple-element.44), channel_id=1, source_target_pairs={{0,8},{2,10},{4,12},{6,14},{8,0},{10,2},{12,4},{14,6},{1,9},{3,11}... | collective-permute-start | bytes 196616 | tf_op jit(solution)/shard_map/ppermute | solution.py:26
  58.9 4.8 %collective-permute-start.17 = (bf16[1,128,256]{2,1,0:T(8,128)(2,1)S(1)}, bf16[1,128,256]{2,1,0:T(8,128)(2,1)S(1)}, u32[]{:S(2)}, u32[]{:S(2)}) collective-permute-start(bf16[1,128,256]{2,1,0:T(8,128)(2,1)S(1)} %get-tuple-element.47), channel_id=1, source_target_pairs={{0,2},{2,0},{4,6},{6,4},{8,10},{10,8},{12,14},{14,12},{1,3},{3,1},... | collective-permute-start | bytes 196616 | tf_op jit(solution)/shard_map/ppermute | solution.py:26
  63.6 4.3 %collective-permute-start.18 = (bf16[1,128,256]{2,1,0:T(8,128)(2,1)S(1)}, bf16[1,128,256]{2,1,0:T(8,128)(2,1)S(1)}, u32[]{:S(2)}, u32[]{:S(2)}) collective-permute-start(bf16[1,128,256]{2,1,0:T(8,128)(2,1)S(1)} %get-tuple-element.46), channel_id=1, source_target_pairs={{0,4},{2,6},{4,0},{6,2},{8,12},{10,14},{12,8},{14,10},{1,5},{3,7},... | collective-permute-start | bytes 196616 | tf_op jit(solution)/shard_map/ppermute | solution.py:26
  67.9 5.2 %collective-permute-start.19 = (bf16[1,128,256]{2,1,0:T(8,128)(2,1)S(1)}, bf16[1,128,256]{2,1,0:T(8,128)(2,1)S(1)}, u32[]{:S(2)}, u32[]{:S(2)}) collective-permute-start(bf16[1,128,256]{2,1,0:T(8,128)(2,1)S(1)} %get-tuple-element.45), channel_id=1, source_target_pairs={{0,6},{2,4},{4,2},{6,0},{8,14},{10,12},{12,10},{14,8},{1,7},{3,5},... | collective-permute-start | bytes 196616 | tf_op jit(solution)/shard_map/ppermute | solution.py:26
  81.3 4.1 %collective-permute-start.7 = (bf16[2,8,128,256]{3,2,1,0:T(8,128)(2,1)}, bf16[2,8,128,256]{3,2,1,0:T(8,128)(2,1)}, u32[]{:S(2)}, u32[]{:S(2)}) collective-permute-start(bf16[2,8,128,256]{3,2,1,0:T(8,128)(2,1)} %pad_maximum_fusion), channel_id=1, source_target_pairs={{0,1},{1,0},{2,3},{3,2},{4,5},{5,4},{6,7},{7,6},{8,9},{9,8},{10,11... | collective-permute-start | bytes 3145736 | tf_op jit(solution)/shard_map/ppermute | solution.py:34
  82.4 4.7 %collective-permute-start.15 = (bf16[2,8,128,256]{3,2,1,0:T(8,128)(2,1)}, bf16[2,8,128,256]{3,2,1,0:T(8,128)(2,1)}, u32[]{:S(2)}, u32[]{:S(2)}) collective-permute-start(bf16[2,8,128,256]{3,2,1,0:T(8,128)(2,1)} %pad_maximum_fusion.1), channel_id=1, source_target_pairs={{0,1},{1,0},{2,3},{3,2},{4,5},{5,4},{6,7},{7,6},{8,9},{9,8},{10,11... | collective-permute-start | bytes 3145736 | tf_op jit(solution)/shard_map/ppermute | solution.py:34
  85.4 3.4 %collective-permute-start.24 = (bf16[2,8,128,256]{3,2,1,0:T(8,128)(2,1)S(1)}, bf16[2,8,128,256]{3,2,1,0:T(8,128)(2,1)S(1)}, u32[]{:S(2)}, u32[]{:S(2)}) collective-permute-start(bf16[2,8,128,256]{3,2,1,0:T(8,128)(2,1)S(1)} %pad_maximum_fusion.2), channel_id=1, source_target_pairs={{0,1},{1,0},{2,3},{3,2},{4,5},{5,4},{6,7},{7,6},{8,9},{9,8},{10,11... | collective-permute-start | bytes 3145736 | tf_op jit(solution)/shard_map/ppermute | solution.py:34
  93.3 3.2 %collective-permute-start.16 = (bf16[1024,512]{1,0:T(8,128)(2,1)S(1)}, bf16[1024,512]{1,0:T(8,128)(2,1)S(1)}, u32[]{:S(2)}, u32[]{:S(2)}) collective-permute-start(bf16[1024,512]{1,0:T(8,128)(2,1)S(1)} %convolution_convert_fusion.2), channel_id=1, source_target_pairs={{0,1},{1,0},{2,3},{3,2},{4,5},{5,4},{6,7},{7,6},{8,9},{9,8},{10,11... | collective-permute-start | bytes 3145736 | tf_op jit(solution)/shard_map/ppermute | solution.py:34
  94.6 3.0 %collective-permute-start.26 = (bf16[1024,512]{1,0:T(8,128)(2,1)S(1)}, bf16[1024,512]{1,0:T(8,128)(2,1)S(1)}, u32[]{:S(2)}, u32[]{:S(2)}) collective-permute-start(bf16[1024,512]{1,0:T(8,128)(2,1)S(1)} %convolution_convert_fusion), channel_id=1, source_target_pairs={{0,1},{1,0},{2,3},{3,2},{4,5},{5,4},{6,7},{7,6},{8,9},{9,8},{10,11... | collective-permute-start | bytes 3145736 | tf_op jit(solution)/shard_map/ppermute | solution.py:34
  96.0 3.1 %collective-permute-start.25 = (bf16[1024,512]{1,0:T(8,128)(2,1)S(1)}, bf16[1024,512]{1,0:T(8,128)(2,1)S(1)}, u32[]{:S(2)}, u32[]{:S(2)}) collective-permute-start(bf16[1024,512]{1,0:T(8,128)(2,1)S(1)} %convolution_convert_fusion.1), channel_id=1, source_target_pairs={{0,1},{1,0},{2,3},{3,2},{4,5},{5,4},{6,7},{7,6},{8,9},{9,8},{10,11... | collective-permute-start | bytes 3145736 | tf_op jit(solution)/shard_map/ppermute | solution.py:34
  102.7 20.2 %all-to-all-start.2 = ((bf16[8,128,256]{2,1,0:T(8,128)(2,1)}), bf16[8,128,256]{2,1,0:T(8,128)(2,1)S(1)}, u32[]{:S(2)}, u32[]{:S(2)}) async-start(bf16[8,128,256]{2,1,0:T(8,128)(2,1)} %copy.100), calls=%async_computation.2 | async-start | bytes 1048576 | tf_op jit(solution)/shard_map/all_to_all | solution.py:131
  122.9 18.3 %all-to-all-start = ((bf16[8,128,256]{2,1,0:T(8,128)(2,1)}), bf16[8,128,256]{2,1,0:T(8,128)(2,1)S(1)}, u32[]{:S(2)}, u32[]{:S(2)}) async-start(bf16[8,128,256]{2,1,0:T(8,128)(2,1)} %copy.84), calls=%async_computation | async-start | bytes 1048576 | tf_op jit(solution)/shard_map/all_to_all | solution.py:131
  141.2 18.3 %all-to-all-start.1 = ((bf16[8,128,256]{2,1,0:T(8,128)(2,1)}), bf16[8,128,256]{2,1,0:T(8,128)(2,1)S(1)}, u32[]{:S(2)}, u32[]{:S(2)}) async-start(bf16[8,128,256]{2,1,0:T(8,128)(2,1)} %copy.98), calls=%async_computation.1 | async-start | bytes 1048576 | tf_op jit(solution)/shard_map/all_to_all | solution.py:131
